TPU v7x, 32 devices: a whole 2x2x4 slice. The times are simulated.
32 devices in a mesh: gx: 16 (over z, x, core), gy: 2 (over y).
Axes of the slice: x: 2, y: 2, z: 4, core: 2. Of those that a mesh axis runs over, the one named last changes fastest.
Arguments:
- potential: float32 [3, 1, 4096, 256], P(None, None, 'gx', 'gy'), may hold values from -8 to 8
- labels: int32 [1, 4096, 256], P(None, 'gx', 'gy'), may hold values from 0 to 7
- principal: float32 [2, 8], replicated, may hold values from 0.5 to 16
- off_diagonal: float32 [3, 8], replicated, may hold values from -0.4 to 0.4
Outputs:
- updated: float32 [3, 1, 4096, 256], P(None, None, 'gx', 'gy')
All inputs are finite; a program needn't handle non-finite values.
Results may differ from a plain program's by a relative error of at most 0.0017.
Values sent between devices are 32-bit elements; how exact they have to be, the bound alone decides.
A program may use at most 64 MiB of HBM per device.

v0:
```python
import jax
import jax.numpy as jnp
from jax import lax
from jax.sharding import PartitionSpec as P


def shifted_2(shard, axis, by):
    size = lax.axis_size(axis)
    return lax.ppermute(shard, axis, [(i, (i + by) % size) for i in range(size)])


def padded_2(cells, sides, width):
    for axis, dim in sides:
        count = lax.axis_size(axis)
        head = lax.slice_in_dim(cells, 0, width, axis=dim)
        tail = lax.slice_in_dim(cells, cells.shape[dim] - width, cells.shape[dim], axis=dim)
        cells = jnp.concatenate(
            [
                lax.ppermute(tail, axis, [(i, (i + 1) % count) for i in range(count)]),
                cells,
                lax.ppermute(head, axis, [((i + 1) % count, i) for i in range(count)]),
            ],
            axis=dim,
        )
    return cells


def harmonic(first, second):
    return 2.0 * first * second / (first + second)


def neighbour(values, offset, axis_dim, filler):
    extent = values.shape[axis_dim]
    dims_pad = list(values.shape)
    dims_pad[axis_dim] = abs(offset)
    padding = jnp.full(tuple(dims_pad), filler, values.dtype)
    if offset > 0:
        retained = lax.slice_in_dim(values, 0, extent - offset, axis=axis_dim)
        return jnp.concatenate([padding, retained], axis_dim)
    retained = lax.slice_in_dim(values, -offset, extent, axis=axis_dim)
    return jnp.concatenate([retained, padding], axis_dim)


def shifted(values, offset, axis_dim, wrap, filler):
    if wrap:
        return jnp.roll(values, offset, axis_dim)
    return neighbour(values, offset, axis_dim, filler)


def cyclic_reduce(sub_diag, main_diag, super_diag, forcing, axis_dim, wrap):
    extent = sub_diag.shape[axis_dim]
    stride = 1
    while stride < extent:
        low_before = shifted(sub_diag, stride, axis_dim, wrap, 0.0)
        main_before = shifted(main_diag, stride, axis_dim, wrap, 1.0)
        high_before = shifted(super_diag, stride, axis_dim, wrap, 0.0)
        rest_before = shifted(forcing, stride, axis_dim + 1, wrap, 0.0)
        low_after = shifted(sub_diag, -stride, axis_dim, wrap, 0.0)
        main_after = shifted(main_diag, -stride, axis_dim, wrap, 1.0)
        high_after = shifted(super_diag, -stride, axis_dim, wrap, 0.0)
        rest_after = shifted(forcing, -stride, axis_dim + 1, wrap, 0.0)
        factor_low = -sub_diag / main_before
        factor_high = -super_diag / main_after
        forcing = forcing + factor_low[None] * rest_before + factor_high[None] * rest_after
        main_diag = main_diag + factor_low * high_before + factor_high * low_after
        sub_diag = factor_low * low_before
        super_diag = factor_high * high_after
        stride = stride * 2
    return forcing / (sub_diag + main_diag + super_diag)[None]


def reduced_rows(tail_row, next_head, low_last, main_last, high_last, force_last):
    reduced_low = -low_last * tail_row[3]
    reduced_main = main_last - low_last * tail_row[4] - high_last * next_head[3]
    reduced_high = -high_last * next_head[4]
    reduced_force = force_last - low_last[None] * tail_row[:3] - high_last[None] * next_head[:3]
    return jnp.concatenate(
        [reduced_low[None], reduced_main[None], reduced_high[None], reduced_force], 0
    )


def spike_solve(sub_diag, main_diag, super_diag, forcing, axis_dim, interface):
    length = sub_diag.shape[axis_dim]
    position = lax.broadcasted_iota(jnp.int32, sub_diag.shape, axis_dim)
    is_last = position == length - 1
    low_inner = jnp.where((position == 0) | is_last, 0.0, sub_diag)
    high_inner = jnp.where((position == length - 2) | is_last, 0.0, super_diag)
    main_inner = jnp.where(is_last, 1.0, main_diag)
    left_spike = jnp.where(position == 0, sub_diag, 0.0)
    right_spike = jnp.where(position == length - 2, super_diag, 0.0)
    stacked = jnp.concatenate(
        [jnp.where(is_last[None], 0.0, forcing), left_spike[None], right_spike[None]], 0
    )
    solved = cyclic_reduce(low_inner, main_inner, high_inner, stacked, axis_dim, False)
    head_row = lax.slice_in_dim(solved, 0, 1, axis=axis_dim + 1)
    tail_row = lax.slice_in_dim(solved, length - 2, length - 1, axis=axis_dim + 1)
    low_last = lax.slice_in_dim(sub_diag, length - 1, length, axis=axis_dim)
    main_last = lax.slice_in_dim(main_diag, length - 1, length, axis=axis_dim)
    high_last = lax.slice_in_dim(super_diag, length - 1, length, axis=axis_dim)
    force_last = lax.slice_in_dim(forcing, length - 1, length, axis=axis_dim + 1)
    own_value, prev_value = interface(
        head_row, tail_row, low_last, main_last, high_last, force_last
    )
    inner_values = solved[:3] - solved[3][None] * prev_value - solved[4][None] * own_value
    return jnp.where(is_last[None], own_value, inner_values)


def pick_values(solution, members, my_index, axis_dim):
    own_value = lax.dynamic_slice_in_dim(solution, my_index, 1, axis_dim)
    prev_value = lax.dynamic_slice_in_dim(solution, (my_index + members - 1) % members, 1, axis_dim)
    return (own_value, prev_value)


def interface_x(head_row, tail_row, low_last, main_last, high_last, force_last):
    members = lax.axis_size("gx")
    my_index = lax.axis_index("gx")
    next_head = shifted_2(head_row, "gx", -1)
    rows_here = reduced_rows(tail_row, next_head, low_last, main_last, high_last, force_last)
    gathered = lax.all_gather(rows_here, "gx", axis=2, tiled=True)
    solution = cyclic_reduce(gathered[0], gathered[1], gathered[2], gathered[3:], 1, True)
    return pick_values(solution, members, my_index, 2)


def interface_y(head_row, tail_row, low_last, main_last, high_last, force_last):
    members = lax.axis_size("gy")
    next_head = shifted_2(head_row, "gy", -1)
    rows_here = reduced_rows(tail_row, next_head, low_last, main_last, high_last, force_last)
    gathered = lax.all_gather(rows_here, "gy", axis=3, tiled=True)
    solution = cyclic_reduce(gathered[0], gathered[1], gathered[2], gathered[3:], 2, True)
    return pick_values(solution, members, lax.axis_index("gy"), 3)


def lookup_phase(components, label_block):
    cell_tensor = jnp.zeros((5,) + label_block.shape, jnp.float32)
    for phase_id in range(components.shape[1]):
        cell_tensor = jnp.where(
            (label_block == phase_id)[None],
            components[:, phase_id][:, None, None, None],
            cell_tensor,
        )
    return cell_tensor


def local(potential, labels, principal, off_diagonal):
    components = jnp.concatenate([principal, off_diagonal], 0)
    cell_tensor = lookup_phase(components, labels)
    padded = padded_2(cell_tensor, (("gx", 2), ("gy", 3)), 1)
    damping = 2.0 / (potential.shape[3] * potential.shape[3])
    along_xdir = padded[:, :, :, 1:-1]
    cond_xx = along_xdir[0]
    face_east = harmonic(cond_xx[:, 1:-1], cond_xx[:, 2:])
    face_west = harmonic(cond_xx[:, :-2], cond_xx[:, 1:-1])
    source_x = jnp.stack(
        [
            face_east - face_west,
            0.5 * (along_xdir[2][:, 2:] - along_xdir[2][:, :-2]),
            0.5 * (along_xdir[3][:, 2:] - along_xdir[3][:, :-2]),
        ]
    )
    half_step = spike_solve(
        -face_west,
        damping + face_west + face_east,
        -face_east,
        damping * potential + source_x,
        1,
        interface_x,
    )
    along_ydir = padded[:, :, 1:-1, :]
    cond_yy = along_ydir[1]
    face_north = harmonic(cond_yy[:, :, 1:-1], cond_yy[:, :, 2:])
    face_south = harmonic(cond_yy[:, :, :-2], cond_yy[:, :, 1:-1])
    source_y = jnp.stack(
        [
            0.5 * (along_ydir[2][:, :, 2:] - along_ydir[2][:, :, :-2]),
            face_north - face_south,
            0.5 * (along_ydir[4][:, :, 2:] - along_ydir[4][:, :, :-2]),
        ]
    )
    return spike_solve(
        -face_south,
        damping + face_south + face_north,
        -face_north,
        damping * half_step + source_y,
        2,
        interface_y,
    )


def solution(mesh):
    in_specs = (P(None, None, "gx", "gy"), P(None, "gx", "gy"), P(), P())
    out_specs = P(None, None, "gx", "gy")
    return jax.shard_map(local, mesh=mesh, in_specs=in_specs, out_specs=out_specs, check_vma=False)
```

profile of v0, /device:TPU:0, one launch (start us, length us, event | category | flops | bytes accessed | tf_op | source)
XLA Modules:
  0.0 70.5 jit_solution(12789829236502406646)
XLA Ops:
  0.0 0.7 pad_maximum_fusion.15
  0.7 0.3 slice_reduce_fusion.9
  1.0 1.1 %compare_bitcast_fusion.7 = (pred[256,128]{1,0:T(8,128)(4,1)S(1)}, pred[256,128]{1,0:T(8,128)(4,1)S(1)}, pred[256,128]{1,0:T(8,128)(4,1)S(1)}, pred[256,128]{1,0...) fusion(s32[1,256,128]{2,1,0:T(8,128)} %param.5), kind=kLoop, calls=%fused_computation.147 | loop fusion | flops 262144 | bytes 393216 | tf_op jit(solution)/shard_map/jit(_where)/broadcast_in_dim | solution.py:136
  3.1 0.3 select_select_fusion
  3.4 0.2 fusion.132
  3.6 5.5 %collective-permute-start.1 = (f32[5,1,1,128]{2,3,1,0:T(8,128)S(1)}, f32[5,1,1,128]{2,3,1,0:T(8,128)S(1)}, u32[]{:S(2)}, u32[]{:S(2)}) collective-permute-start(f32[5,1,1,128]{2,3,1,0:T(8,128)S(1)} %get-tuple-element.150), channel_id=1, source_target_pairs={{2,0},{4,2},{6,4},{8,6},{10,8},{12,10},{14,12},{16,14},{18,16},{20... | collective-permute-start | bytes 7688 | tf_op jit(solution)/shard_map/ppermute | solution.py:21
  9.0 0.6 iota_compare_fusion.5
  9.6 0.6 fusion.77
  10.2 0.5 iota_compare_fusion.4
  10.7 0.5 iota_compare_fusion.3
  11.2 0.6 fusion.76
  11.9 0.2 copy.135
  12.1 1.6 %collective-permute-done.1 = f32[5,1,1,128]{2,3,1,0:T(8,128)S(1)} collective-permute-done((f32[5,1,1,128]{2,3,1,0:T(8,128)S(1)}, f32[5,1,1,128]{2,3,1,0:T(8,128)S(1)}, u32[]{:S(2)}, u32[]{:S(2)}) %collective-permute-start.1) | collective-permute-done | bytes 2592 | tf_op jit(solution)/shard_map/ppermute | solution.py:21
  13.6 4.6 %collective-permute-done = f32[5,1,1,128]{2,3,1,0:T(8,128)S(1)} collective-permute-done((f32[5,1,1,128]{2,3,1,0:T(8,128)S(1)}, f32[5,1,1,128]{2,3,1,0:T(8,128)S(1)}, u32[]{:S(2)}, u32[]{:S(2)}) %collective-permute-start) | collective-permute-done | bytes 2592 | tf_op jit(solution)/shard_map/ppermute | solution.py:19
  18.2 0.3 maximum_bitcast_fusion
  18.5 0.1 fusion.116
  18.7 0.7 broadcast_select_fusion.3
  19.9 0.2 fusion.131
  20.1 0.3 multiply_add_fusion.12
  20.4 0.2 fusion.130
  20.9 0.1 multiply_add_fusion.25
  21.2 0.2 fusion.90
  21.4 0.3 multiply_add_fusion.11
  21.6 0.2 fusion.129
  22.1 0.1 multiply_add_fusion.24
  22.4 0.2 fusion.92
  22.6 0.3 multiply_add_fusion.10
  22.9 0.2 fusion.128
  23.6 0.2 fusion.94
  23.8 0.3 multiply_add_fusion.9
  24.1 0.2 fusion.127
  24.8 0.2 fusion.96
  25.0 0.3 multiply_add_fusion.8
  25.3 0.2 fusion.126
  26.0 0.2 fusion.98
  26.2 0.3 multiply_add_fusion.7
  26.5 0.2 fusion.125
  27.3 0.2 fusion.100
  27.4 0.3 multiply_add_fusion.6
  28.0 0.1 multiply_add_fusion.19
  28.6 0.2 collective-permute-start.4
  28.8 0.7 %pad_maximum_fusion.13 = (f32[5,1,258,1]{2,3,1,0:T(1,128)}, f32[5,1,258,1]{2,3,1,0:T(1,128)}) fusion(f32[5,1,1,128]{2,3,1,0:T(8,128)S(1)} %collective-permute-done.1, f32[5,1,256,128]{2,3,1,0:T(8,128)S(1)} %select_select_fusion, f32[5,1,1,128]{2,3,1,0:T(8,128)S(1)} %collective-permute-done), kind=kLoop, calls=%fused_computation.248 | loop fusion | flops 5160 | bytes 670800 | tf_op jit(solution)/shard_map/slice | solution.py:16
  29.6 1.6 %collective-permute-start.3 = (f32[5,1,258,1]{2,3,1,0:T(1,128)}, f32[5,1,258,1]{2,3,1,0:T(1,128)S(1)}, u32[]{:S(2)}, u32[]{:S(2)}) collective-permute-start(f32[5,1,258,1]{2,3,1,0:T(1,128)} %get-tuple-element.112), channel_id=1, source_target_pairs={{1,0},{0,1},{3,2},{2,3},{5,4},{4,5},{7,6},{6,7},{9,8},{8,9},{11,10... | collective-permute-start | bytes 15488 | tf_op jit(solution)/shard_map/ppermute | solution.py:21
  31.2 0.5 collective-permute-start.2
  31.8 0.6 copy.142
  32.5 0.8 %collective-permute-done.4 = f32[5,1,1,128]{2,3,1,0:T(8,128)S(1)} collective-permute-done((f32[5,1,1,128]{2,3,1,0:T(8,128)S(1)}, f32[5,1,1,128]{2,3,1,0:T(8,128)S(1)}, u32[]{:S(2)}, u32[]{:S(2)}) %collective-permute-start.4) | collective-permute-done | bytes 2592 | tf_op jit(solution)/shard_map/ppermute | solution.py:9
  33.5 0.8 %copy-done.1 = f32[1,256,128]{1,2,0:T(8,128)S(1)} copy-done((f32[1,256,128]{1,2,0:T(8,128)S(1)}, f32[1,256,128]{1,2,0:T(8,128)}, u32[]{:S(2)}) %copy-start.1) | copy-done | bytes 131096
  34.3 0.3 fusion.24
  34.6 0.6 copy-done.2
  35.2 18.7 %all_gather.6 = f32[6,1,16,128]{3,1,0,2:T(1,128)S(1)} all-gather(f32[6,1,1,128]{3,1,0,2:T(1,128)S(1)} %maximum_bitcast_fusion.5), channel_id=1, replica_groups=mesh['gx'=16,'gy'=2] {'gx'}, dimensions={2}, use_global_device_ids=true | all-gather | bytes 52224 | tf_op jit(solution)/shard_map/all_gather | solution.py:119
  55.2 0.7 copy-done.3
  56.0 0.6 copy-done.9
  56.7 0.1 fusion.102
  56.8 0.7 copy-done.5
  57.5 0.2 broadcast_select_fusion
  57.9 0.2 multiply_add_fusion.5
  58.4 0.2 multiply_add_fusion.4
  59.0 0.2 multiply_add_fusion.3
  59.5 0.2 multiply_add_fusion.2
  60.1 0.1 multiply_add_fusion.1
  61.2 1.6 %collective-permute-start.5 = (f32[5,1,256,1]{2,3,1,0:T(1,128)S(1)}, f32[5,1,256,1]{2,3,1,0:T(1,128)S(1)}, u32[]{:S(2)}, u32[]{:S(2)}) collective-permute-start(f32[5,1,256,1]{2,3,1,0:T(1,128)S(1)} %slice.1303), channel_id=1, source_target_pairs={{0,1},{1,0},{2,3},{3,2},{4,5},{5,4},{6,7},{7,6},{8,9},{9,8},{10,11... | collective-permute-start | bytes 15368 | tf_op jit(solution)/shard_map/ppermute | solution.py:9
  62.8 2.1 %collective-permute-done.5 = f32[5,1,256,1]{2,3,1,0:T(1,128)S(1)} collective-permute-done((f32[5,1,256,1]{2,3,1,0:T(1,128)S(1)}, f32[5,1,256,1]{2,3,1,0:T(1,128)S(1)}, u32[]{:S(2)}, u32[]{:S(2)}) %collective-permute-start.5) | collective-permute-done | bytes 5152 | tf_op jit(solution)/shard_map/ppermute | solution.py:9
  65.0 4.4 %all_gather.7 = f32[6,1,256,2]{2,1,0,3:T(1,128)S(1)} all-gather(f32[6,1,256,1]{2,1,0,3:T(1,128)S(1)} %maximum_bitcast_fusion.4), channel_id=1, replica_groups=mesh['gx'=16,'gy'=2] {'gy'}, dimensions={3}, use_global_device_ids=true | all-gather | bytes 18432 | tf_op jit(solution)/shard_map/all_gather | solution.py:128
  69.6 0.9 %copy.153 = f32[3,1,256,128]{3,2,1,0:T(8,128)} copy(f32[3,1,256,128]{2,3,1,0:T(8,128)S(1)} %fusion.1) | data formatting | bytes 786432 | tf_op jit(solution)/shard_map/jit(_where)/select_n | solution.py:105
  (197 shorter events, 8.9 us)
Async XLA Ops:
  3.4 8.5 %copy-start = (f32[3,1,256,128]{3,2,1,0:T(8,128)S(1)}, f32[3,1,256,128]{3,2,1,0:T(8,128)}, u32[]{:S(2)}) copy-start(f32[3,1,256,128]{3,2,1,0:T(8,128)} %param.4) | copy-start | bytes 1179652
  3.6 10.1 %collective-permute-start.1 = (f32[5,1,1,128]{2,3,1,0:T(8,128)S(1)}, f32[5,1,1,128]{2,3,1,0:T(8,128)S(1)}, u32[]{:S(2)}, u32[]{:S(2)}) collective-permute-start(f32[5,1,1,128]{2,3,1,0:T(8,128)S(1)} %get-tuple-element.150), channel_id=1, source_target_pairs={{2,0},{4,2},{6,4},{8,6},{10,8},{12,10},{14,12},{16,14},{18,16},{20... | collective-permute-start | bytes 7688 | tf_op jit(solution)/shard_map/ppermute | solution.py:21
  9.0 9.2 %collective-permute-start = (f32[5,1,1,128]{2,3,1,0:T(8,128)S(1)}, f32[5,1,1,128]{2,3,1,0:T(8,128)S(1)}, u32[]{:S(2)}, u32[]{:S(2)}) collective-permute-start(f32[5,1,1,128]{2,3,1,0:T(8,128)S(1)} %get-tuple-element.149), channel_id=1, source_target_pairs={{0,2},{2,4},{4,6},{6,8},{8,10},{10,12},{12,14},{14,16},{16,18},{18... | collective-permute-start | bytes 7688 | tf_op jit(solution)/shard_map/ppermute | solution.py:19
  11.8 7.9 %copy-start.4 = (pred[256]{0:T(512)(128)(4,1)}, pred[256]{0:T(512)(128)(4,1)S(1)}, u32[]{:S(2)}) copy-start(pred[256]{0:T(512)(128)(4,1)S(1)} %iota_compare_fusion.2) | copy-start | bytes 772
  28.6 4.8 %collective-permute-start.4 = (f32[5,1,1,128]{2,3,1,0:T(8,128)S(1)}, f32[5,1,1,128]{2,3,1,0:T(8,128)S(1)}, u32[]{:S(2)}, u32[]{:S(2)}) collective-permute-start(f32[5,1,1,128]{2,3,1,0:T(8,128)S(1)} %slice.1169), channel_id=1, source_target_pairs={{0,30},{2,0},{4,2},{6,4},{8,6},{10,8},{12,10},{14,12},{16,14},{18,... | collective-permute-start | bytes 7688 | tf_op jit(solution)/shard_map/ppermute | solution.py:9
  29.6 25.3 %collective-permute-start.3 = (f32[5,1,258,1]{2,3,1,0:T(1,128)}, f32[5,1,258,1]{2,3,1,0:T(1,128)S(1)}, u32[]{:S(2)}, u32[]{:S(2)}) collective-permute-start(f32[5,1,258,1]{2,3,1,0:T(1,128)} %get-tuple-element.112), channel_id=1, source_target_pairs={{1,0},{0,1},{3,2},{2,3},{5,4},{4,5},{7,6},{6,7},{9,8},{8,9},{11,10... | collective-permute-start | bytes 15488 | tf_op jit(solution)/shard_map/ppermute | solution.py:21
  31.2 23.7 %collective-permute-start.2 = (f32[5,1,258,1]{2,3,1,0:T(1,128)}, f32[5,1,258,1]{2,3,1,0:T(1,128)S(1)}, u32[]{:S(2)}, u32[]{:S(2)}) collective-permute-start(f32[5,1,258,1]{2,3,1,0:T(1,128)} %get-tuple-element.111), channel_id=1, source_target_pairs={{0,1},{1,0},{2,3},{3,2},{4,5},{5,4},{6,7},{7,6},{8,9},{9,8},{10,11... | collective-permute-start | bytes 15488 | tf_op jit(solution)/shard_map/ppermute | solution.py:19
  33.4 0.9 %copy-start.1 = (f32[1,256,128]{1,2,0:T(8,128)S(1)}, f32[1,256,128]{1,2,0:T(8,128)}, u32[]{:S(2)}) copy-start(f32[1,256,128]{1,2,0:T(8,128)} %get-tuple-element.102) | copy-start | bytes 393220
  34.6 0.6 copy-start.2
  55.2 0.7 copy-start.3
  55.9 0.7 copy-start.9
  56.0 0.7 copy-start.6
  56.0 0.7 copy-start.7
  56.0 0.6 copy-start.8
  56.8 0.7 copy-start.5
  61.2 3.7 %collective-permute-start.5 = (f32[5,1,256,1]{2,3,1,0:T(1,128)S(1)}, f32[5,1,256,1]{2,3,1,0:T(1,128)S(1)}, u32[]{:S(2)}, u32[]{:S(2)}) collective-permute-start(f32[5,1,256,1]{2,3,1,0:T(1,128)S(1)} %slice.1303), channel_id=1, source_target_pairs={{0,1},{1,0},{2,3},{3,2},{4,5},{5,4},{6,7},{7,6},{8,9},{9,8},{10,11... | collective-permute-start | bytes 15368 | tf_op jit(solution)/shard_map/ppermute | solution.py:9
where the time goes:
time: 70.8 us; the launch traced here: 70.5 us
  blocking collectives  23.1 us (33%)
  other arithmetic  15.5 us (22%)
  local copies, waits for them, and re-layouts  12 us (17%)
  starting transfers between devices  9.31 us (13%)
  waiting for transfers between devices  9.1 us (13%)
  between operations  1.55 us (2%)
    all_gather x1, blocking collectives, interface_x(): gathered = lax.all_gather(rows_here, 'gx', axis=2, tiled=True)  18.7 us
    ppermute x2, starting transfers between devices, padded_2(): lax.ppermute(head, axis, [((i + 1) % count, i) for i in range(count)])  7.05 us
    ppermute x2, waiting for transfers between devices, padded_2(): lax.ppermute(tail, axis, [(i, (i + 1) % count) for i in range(count)])  4.61 us
    all_gather x1, blocking collectives, interface_y(): gathered = lax.all_gather(rows_here, 'gy', axis=3, tiled=True)  4.36 us
    slice x47, local copies, waits for them, and re-layouts, neighbour(): retained = lax.slice_in_dim(values, 0, extent - offset, axis=axis_dim)  3.91 us
    unnamed x28, local copies, waits for them, and re-layouts  3.57 us
    add x16, other arithmetic, cyclic_reduce(): forcing + factor_low[None] * rest_before + factor_high[None] * rest_after  3.03 us
    ppermute x2, waiting for transfers between devices, shifted_2(): lax.ppermute(shard, axis, [(i, (i + by) % size) for i in range(size)])  2.92 us
  transfers between devices with their start and end apart: 6, of which 4 were waited for; matrix products, arithmetic and copies ran while one was open for 8% of the time, Pallas kernels for 0%

commit v1 on v0

v1 whole, which is shorter than its diff:
```python
import functools

import jax
import jax.numpy as jnp
from jax import lax
from jax.experimental import pallas as pl
from jax.experimental.pallas import tpu as pltpu
from jax.sharding import PartitionSpec as P

MESH = pl.DeviceIdType.MESH
ROWS = 16


def sublane(shape):
    return lax.broadcasted_iota(jnp.int32, shape, len(shape) - 2)


def turn(x, by):
    size = x.shape[0]
    by = by % size
    return x if by == 0 else pltpu.roll(x, by, 0)


def following(q, last):
    wrap = turn(q[0], -1)
    wrap = jnp.where(sublane(wrap.shape) == 7, last, wrap)
    return wrap[None] if q.shape[0] == 1 else jnp.concatenate([q[1:], wrap[None]], 0)


def preceding(q):
    wrap = turn(q[-1], 1)
    first = jnp.where(sublane(wrap.shape) == 0, 0.0, wrap)[None]
    return (first if q.shape[0] == 1 else jnp.concatenate([first, q[:-1]], 0)), wrap


def split(q):
    pairs = q.reshape((q.shape[0] // 2, 2) + q.shape[1:])
    return pairs[:, 0], pairs[:, 1]


def merge(even, odd):
    return jnp.stack([even, odd], 1).reshape((2 * even.shape[0],) + even.shape[1:])


def wide(parts):
    return parts[0] if len(parts) == 1 else jnp.concatenate(parts, -1)


def strided(ref, steps):
    return jnp.stack([ref[pl.ds(t, 8, stride=steps), :] for t in range(steps)], 0)


def strided_wide(ref, steps):
    return wide([strided(ref.at[c], steps) for c in range(ref.shape[0])])


def put_wide(ref, value):
    for c in range(ref.shape[0]):
        ref[c] = value[:, c * 128 : (c + 1) * 128]


def lookup(tab, row, labels):
    out = jnp.full(labels.shape, tab(row, 0), jnp.float32)
    for phase in range(1, 8):
        out = jnp.where(labels == phase, tab(row, phase), out)
    return out


def faces(k):
    nxt = following(k, k[0])
    e = 2.0 * k * nxt / (k + nxt)
    steps = k.shape[0]
    position = lax.broadcasted_iota(jnp.int32, k.shape, 0)
    return jnp.where((position == steps - 1) & (sublane(k.shape) == 7), 0.0, e)


def factor(e, damping):
    g = jnp.full(e.shape, damping, jnp.float32)
    levels = []
    g_end = jnp.zeros(e.shape[1:], jnp.float32)
    top = True
    while e.shape[0] > 1:
        e_even, e_odd = split(e)
        g_even, g_odd = split(g)
        r = 1.0 / (e_even + e_odd + g_odd)
        if top:
            is_end = (lax.broadcasted_iota(jnp.int32, r.shape, 0) == r.shape[0] - 1) & (sublane(r.shape) == 7)
            r = jnp.where(is_end, 0.0, r)
            right = jnp.where(is_end, 1.0, e_odd * r)
        else:
            right = e_odd * r
        left = e_even * r
        top = False
        levels.append((left, right, r))
        e = e_even * right
        moved, wrap = preceding(right * g_odd)
        g = g_even + left * g_odd + moved
        g_end = g_end + wrap
    e, g = e[0], g[0]
    sub = sublane(e.shape)
    for by in (1, 2, 4):
        chosen = sub % (2 * by) == by
        e_left = turn(e, by)
        r = jnp.where(chosen, 1.0 / (e_left + e + g), 0.0)
        left, right = e_left * r, e * r
        levels.append((left, right, r))
        e = e * turn(right, -by)
        wrap = turn(right * g, by)
        g = g + turn(left * g, -by) + jnp.where(sub == 0, 0.0, wrap)
        g_end = g_end + wrap
    return levels, e, g, g_end


def forward(levels, f):
    kept = []
    f_end = jnp.zeros(f.shape[1:], jnp.float32)
    for left, right, r in levels[:-3]:
        f_even, f_odd = split(f)
        kept.append(f_odd * r)
        moved, wrap = preceding(right * f_odd)
        f = f_even + left * f_odd + moved
        f_end = f_end + wrap
    f = f[0]
    sub = sublane(f.shape)
    for by, (left, right, r) in zip((1, 2, 4), levels[-3:]):
        kept.append(f * r)
        wrap = turn(right * f, by)
        f = f + turn(left * f, -by) + jnp.where(sub == 0, 0.0, wrap)
        f_end = f_end + wrap
    return kept, f, f_end


def backward(levels, kept, first, last):
    shape = kept[-1].shape
    sub = sublane(shape)
    v = jnp.broadcast_to(first, shape)
    last = jnp.broadcast_to(last, shape)
    for by, (left, right, r), own in zip((4, 2, 1), levels[:-4:-1], kept[:-4:-1]):
        after = jnp.where(sub >= 8 - by, last, turn(v, -by))
        v = jnp.where(sub % (2 * by) == by, own + left * turn(v, by) + right * after, v)
    v = v[None]
    for (left, right, r), own in zip(levels[:-3][::-1], kept[:-3][::-1]):
        odd = own + left * v + right * following(v, last)
        v = merge(v, odd)
    return v


def central(k):
    return 0.5 * (following(k, jnp.zeros_like(k[0])) - preceding(k)[0])


def put_record(box, me, e, g, g_end, fs, f_ends, edges):
    base = pl.multiple_of(me * ROWS, ROWS)
    rows = [e[0:1], g[0:1]] + [f[0:1] for f in fs] + [g_end[0:1]] + [f[0:1] for f in f_ends]
    rows += [k[0, 0:1] for k in edges] + [k[-1, 7:8] for k in edges]
    rows.append(jnp.zeros_like(rows[0]))
    rows = jnp.concatenate(rows, 0)
    for c in range(box.shape[0]):
        box[c, pl.ds(base, ROWS), :] = rows[:, c * 128 : (c + 1) * 128]


def copies(box, me, n, axis, send, recv):
    out = []
    for d in range(1, n):
        slot = box.at[:, pl.ds(pl.multiple_of(me * ROWS, ROWS), ROWS), :]
        out.append(
            pltpu.make_async_remote_copy(
                src_ref=slot,
                dst_ref=slot,
                send_sem=send.at[d],
                recv_sem=recv.at[d],
                device_id={axis: lax.rem(me + d, n)},
                device_id_type=MESH,
            )
        )
    return out


def interface(box, n, order, me, first_out, last_out):
    def get_part(q, c):
        if n >= 8:
            return box[c, pl.ds(q, n, stride=ROWS), :]
        sub = sublane((8, 128)) % n
        out = jnp.broadcast_to(box[c, q : q + 1, :], (8, 128))
        for i in range(1, n):
            out = jnp.where(sub == i, box[c, i * ROWS + q : i * ROWS + q + 1, :], out)
        return out

    def get(q):
        return wide([get_part(q, c) for c in range(box.shape[0])])

    e, g = get(0), get(1)
    f = [get(2 + i) for i in range(3)]
    g_end = get(5)
    f_end = [get(6 + i) for i in range(3)]
    head = [get(9 + i) for i in range(3)]
    tail = [get(12 + i) for i in range(3)]
    head_next = [turn(k, -1) for k in head]
    link = 2.0 * tail[0] * head_next[0] / (tail[0] + head_next[0])
    gain = [link, 0.5 * head_next[1], 0.5 * head_next[2]]
    loss = [turn(link, 1), turn(0.5 * tail[1], 1), turn(0.5 * tail[2], 1)]
    for i, which in enumerate(order):
        f[i] = f[i] - loss[which]
        f_end[i] = f_end[i] + gain[which]
    r = 1.0 / (e + link + g_end)
    left, right = e * r, link * r
    g = g + left * g_end + turn(right * g_end, 1)
    f = [a + left * b + turn(right * b, 1) for a, b in zip(f, f_end)]
    e = e * right
    by = 1
    while by < n:
        e_left = turn(e, by)
        s = 1.0 / (e_left + e + g)
        lo, hi = e_left * s, e * s
        g = g + turn(lo * g, -by) + turn(hi * g, by)
        f = [a + turn(lo * a, -by) + turn(hi * a, by) for a in f]
        e = e * turn(hi, -by)
        by *= 2
    inv = 1.0 / g
    size = g.shape[0]
    for i in range(3):
        v = f[i] * inv
        first_out[i * size : (i + 1) * size, :] = v
        last_out[i * size : (i + 1) * size, :] = r * f_end[i] + left * v + right * turn(v, -1)
    return [
        (first_out[pl.ds(i * size + me, 1), :], last_out[pl.ds(i * size + me, 1), :]) for i in range(3)
    ]


def kernel(nx, ny, damping, pot, lab, pri, off, out, box_x, box_y, labt, ft,
           first_x, last_x, first_y, last_y, send_x, recv_x, send_y, recv_y):
    me_x, me_y = lax.axis_index("gx"), lax.axis_index("gy")
    barrier = pltpu.get_barrier_semaphore()
    for d in range(1, nx):
        pl.semaphore_signal(barrier, inc=1, device_id={"gx": lax.rem(me_x + d, nx)}, device_id_type=MESH)
    for d in range(1, ny):
        pl.semaphore_signal(barrier, inc=1, device_id={"gy": lax.rem(me_y + d, ny)}, device_id_type=MESH)

    def tab(row, phase):
        return pri[row, phase] if row < 2 else off[row - 2, phase]

    rows, cols = lab.shape
    steps = rows // 8
    labels = strided(lab, steps)
    k, a, b = lookup(tab, 0, labels), lookup(tab, 2, labels), lookup(tab, 3, labels)
    e = faces(k)
    levels, e_in, g, g_end = factor(e, damping)
    source = [e - preceding(e)[0], central(a), central(b)]
    solved = [forward(levels, damping * strided(pot.at[i], steps) + source[i]) for i in range(3)]
    put_record(box_x, me_x, e_in, g, g_end, [s[1] for s in solved], [s[2] for s in solved], [k, a, b])
    pl.semaphore_wait(barrier, nx - 1 + ny - 1)
    sent_x = copies(box_x, me_x, nx, "gx", send_x, recv_x)
    for copy in sent_x:
        copy.start()

    lanes = labt.shape[0] * 128
    repeat = lanes // rows

    def across(q):
        flat = q.reshape(rows, cols)
        if repeat > 1:
            flat = jnp.concatenate([flat] * repeat, 0)
        return flat.T

    put_wide(labt, across(labels))
    ysteps = cols // 8
    labels_y = strided_wide(labt, ysteps)
    ky, ay, by = lookup(tab, 1, labels_y), lookup(tab, 2, labels_y), lookup(tab, 4, labels_y)
    ey = faces(ky)
    levels_y, ey_in, gy, gy_end = factor(ey, damping)
    source_y = [central(ay), ey - preceding(ey)[0], central(by)]

    for copy in sent_x:
        copy.wait_recv()
    ends = interface(box_x, nx, (0, 1, 2), me_x, first_x, last_x)
    solved_y = []
    for i in range(3):
        half = backward(levels, solved[i][0], *ends[i])
        put_wide(ft.at[i], across(half))
        solved_y.append(forward(levels_y, damping * strided_wide(ft.at[i], ysteps) + source_y[i]))
    put_record(box_y, me_y, ey_in, gy, gy_end, [s[1] for s in solved_y], [s[2] for s in solved_y], [ky, ay, by])
    sent_y = copies(box_y, me_y, ny, "gy", send_y, recv_y)
    for copy in sent_y:
        copy.start()
    for copy in sent_y:
        copy.wait_recv()
    ends = interface(box_y, ny, (1, 0, 2), me_y, first_y, last_y)
    for i in range(3):
        v = backward(levels_y, solved_y[i][0], *ends[i])
        for t in range(ysteps):
            for c in range(lanes // 128):
                ft[i, c, pl.ds(t, 8, stride=ysteps), :] = v[t, :, c * 128 : (c + 1) * 128]
        back = jnp.concatenate([ft[i, c].T for c in range(lanes // 128)], 0)[:rows].reshape(steps, 8, cols)
        for t in range(steps):
            out[i, pl.ds(t, 8, stride=steps), :] = back[t]
    for copy in sent_x + sent_y:
        copy.wait_send()


def local(potential, labels, principal, off_diagonal):
    nx, ny = lax.axis_size("gx"), lax.axis_size("gy")
    loads, _, rows, cols = potential.shape
    lanes = max(rows, 128)
    damping = 2.0 / (cols * cols)
    vmem = pl.BlockSpec(memory_space=pltpu.VMEM)
    smem = pl.BlockSpec(memory_space=pltpu.SMEM)
    result = pl.pallas_call(
        functools.partial(kernel, nx, ny, damping),
        out_shape=jax.ShapeDtypeStruct((loads, rows, cols), jnp.float32),
        in_specs=[vmem, vmem, smem, smem],
        out_specs=vmem,
        scratch_shapes=[
            pltpu.VMEM((1, nx * ROWS, cols), jnp.float32),
            pltpu.VMEM((lanes // 128, ny * ROWS, 128), jnp.float32),
            pltpu.VMEM((lanes // 128, cols, 128), jnp.int32),
            pltpu.VMEM((loads, lanes // 128, cols, 128), jnp.float32),
            pltpu.VMEM((loads * max(nx, 8), cols), jnp.float32),
            pltpu.VMEM((loads * max(nx, 8), cols), jnp.float32),
            pltpu.VMEM((loads * max(ny, 8), lanes), jnp.float32),
            pltpu.VMEM((loads * max(ny, 8), lanes), jnp.float32),
            pltpu.SemaphoreType.DMA((nx,)),
            pltpu.SemaphoreType.DMA((nx,)),
            pltpu.SemaphoreType.DMA((ny,)),
            pltpu.SemaphoreType.DMA((ny,)),
        ],
        compiler_params=pltpu.CompilerParams(
            collective_id=0, has_side_effects=True, vmem_limit_bytes=32 * 1024 * 1024
        ),
    )(potential.reshape(loads, rows, cols), labels.reshape(rows, cols), principal, off_diagonal)
    return result.reshape(potential.shape)


def solution(mesh):
    in_specs = (P(None, None, "gx", "gy"), P(None, "gx", "gy"), P(), P())
    out_specs = P(None, None, "gx", "gy")
    return jax.shard_map(local, mesh=mesh, in_specs=in_specs, out_specs=out_specs, check_vma=False)
```

time: 70.8 us -> 17.8 us (0.25)
  blocking collectives: 23.1 us -> 0 us
  other arithmetic: 15.5 us -> 0 us
  Pallas kernels: 0 us -> 14.3 us
  starting transfers between devices: 9.31 us -> 0 us
  waiting for transfers between devices: 9.1 us -> 0 us
  local copies, waits for them, and re-layouts: 12 us -> 3.34 us
  between operations: 1.55 us -> 0.01 us
    all_gather x2 -> x0, blocking collectives: 23.1 us -> none  [the longest x1 18.7 us: interface_x(): gathered = lax.all_gather(rows_here, 'gx', axis=2, tiled=True)]
    pallas_call x0 -> x1, Pallas kernels: none -> 14.3 us  [local(): pl.pallas_call(functools.partial(kernel, nx, ny, damping), out_shape=jax....]
    ppermute x6 -> x0, starting transfers between devices: 9.31 us -> none  [the longest x2 7.05 us: padded_2(): lax.ppermute(head, axis, [((i + 1) % count, i) for i in range(count)])]
    ppermute x6 -> x0, waiting for transfers between devices: 9.1 us -> none  [the longest x2 4.61 us: padded_2(): lax.ppermute(tail, axis, [(i, (i + 1) % count) for i in range(count)])]
    slice x84 -> x0, local copies, waits for them, and re-layouts: 6.34 us -> none  [the longest x47 3.91 us: neighbour(): retained = lax.slice_in_dim(values, 0, extent - offset, axis=axis_dim)]
    add x29 -> x0, other arithmetic: 4.43 us -> none  [the longest x16 3.03 us: cyclic_reduce(): forcing + factor_low[None] * rest_before + factor_high[None] * rest_after]
    mul x35 -> x0, other arithmetic: 2.9 us -> none  [the longest x16 1.79 us: cyclic_reduce(): factor_low[None] * rest_before]
    eq x6 -> x0, other arithmetic: 1.63 us -> none  [the longest x2 0.59 us: spike_solve(): is_last = position == length - 1]
  transfers between devices with their start and end apart: 6 -> 0, of which waited for: 4 -> 0; matrix products, arithmetic and copies ran while one was open for 8% -> 0% of each run, Pallas kernels for 0% -> 0%
where the time goes in v1:
time: 17.8 us; the launch traced here: 17.6 us
  Pallas kernels  14.3 us (80%)
  local copies, waits for them, and re-layouts  3.34 us (19%)
    pallas_call x1, Pallas kernels, local(): pl.pallas_call(functools.partial(kernel, nx, ny, damping), out_shape=jax....  14.3 us
    unnamed x9, local copies, waits for them, and re-layouts  3.34 us

profile of v1, /device:TPU:0, one launch (start us, length us, event | category | flops | bytes accessed | tf_op | source)
XLA Modules:
  0.0 17.6 jit_solution(15627196318965418156)
XLA Ops:
  0.0 0.0 copy-start.2
  0.0 0.0 copy-start.3
  0.0 0.7 %copy-done.2 = f32[3,8]{1,0:T(4,128)S(1)} copy-done((f32[3,8]{1,0:T(4,128)S(1)}, f32[3,8]{1,0:T(4,128)}, u32[]{:S(2)}) %copy-start.2) | copy-done | bytes 120
  0.7 0.0 copy-done.3
  0.7 0.0 copy-start
  0.7 1.0 %copy-done = f32[3,1,256,128]{3,2,1,0:T(8,128)S(1)} copy-done((f32[3,1,256,128]{3,2,1,0:T(8,128)S(1)}, f32[3,1,256,128]{3,2,1,0:T(8,128)}, u32[]{:S(2)}) %copy-start) | copy-done | bytes 393240
  1.7 0.0 copy-start.1
  1.7 0.9 %copy-done.1 = s32[1,256,128]{2,1,0:T(8,128)S(1)} copy-done((s32[1,256,128]{2,1,0:T(8,128)S(1)}, s32[1,256,128]{2,1,0:T(8,128)}, u32[]{:S(2)}) %copy-start.1) | copy-done | bytes 131096
  2.6 14.3 %shard_map.46 = f32[3,256,128]{2,1,0:T(8,128)S(1)} custom-call(f32[3,256,128]{2,1,0:T(8,128)S(1)} %bitcast.6, s32[256,128]{1,0:T(8,128)S(1)} %bitcast.7, f32[2,8]{1,0:T(2,128)S(1)} %copy-done.3, f32[3,8]{1,0:T(4,128)S(1)} %copy-done.2), custom_call_target="tpu_custom_call" | custom-call | tf_op jit(solution)/shard_map/pallas_call | solution.py:307
  16.9 0.7 %copy.7 = f32[3,1,256,128]{3,2,1,0:T(8,128)} copy(f32[3,1,256,128]{3,2,1,0:T(8,128)S(1)} %bitcast.5) | data formatting | bytes 786432
Async XLA Ops:
  0.0 0.7 %copy-start.2 = (f32[3,8]{1,0:T(4,128)S(1)}, f32[3,8]{1,0:T(4,128)}, u32[]{:S(2)}) copy-start(f32[3,8]{1,0:T(4,128)} %off.1) | copy-start | bytes 292
  0.0 0.7 %copy-start.3 = (f32[2,8]{1,0:T(2,128)S(1)}, f32[2,8]{1,0:T(2,128)}, u32[]{:S(2)}) copy-start(f32[2,8]{1,0:T(2,128)} %pri.1) | copy-start | bytes 196
  0.7 1.0 %copy-start = (f32[3,1,256,128]{3,2,1,0:T(8,128)S(1)}, f32[3,1,256,128]{3,2,1,0:T(8,128)}, u32[]{:S(2)}) copy-start(f32[3,1,256,128]{3,2,1,0:T(8,128)} %param.4) | copy-start | bytes 1179652
  1.7 0.9 %copy-start.1 = (s32[1,256,128]{2,1,0:T(8,128)S(1)}, s32[1,256,128]{2,1,0:T(8,128)}, u32[]{:S(2)}) copy-start(s32[1,256,128]{2,1,0:T(8,128)} %param.5) | copy-start | bytes 393220

commit v2 on v1

--- a/solution.py
+++ b/solution.py
@@ -8,7 +8,7 @@
 from jax.sharding import PartitionSpec as P
 
 MESH = pl.DeviceIdType.MESH
-ROWS = 16
+ROWS = 8
 
 
 def sublane(shape):
@@ -60,9 +60,9 @@
 
 
 def lookup(tab, row, labels):
-    out = jnp.full(labels.shape, tab(row, 0), jnp.float32)
+    out = jnp.broadcast_to(tab(row, 0), labels.shape)
     for phase in range(1, 8):
-        out = jnp.where(labels == phase, tab(row, phase), out)
+        out = jnp.where(labels == phase, jnp.broadcast_to(tab(row, phase), labels.shape), out)
     return out
 
 
@@ -149,20 +149,26 @@
     return 0.5 * (following(k, jnp.zeros_like(k[0])) - preceding(k)[0])
 
 
-def put_record(box, me, e, g, g_end, fs, f_ends, edges):
-    base = pl.multiple_of(me * ROWS, ROWS)
-    rows = [e[0:1], g[0:1]] + [f[0:1] for f in fs] + [g_end[0:1]] + [f[0:1] for f in f_ends]
-    rows += [k[0, 0:1] for k in edges] + [k[-1, 7:8] for k in edges]
-    rows.append(jnp.zeros_like(rows[0]))
+def put_record(box, me, rows):
+    base = pl.multiple_of(me * len(rows), ROWS)
     rows = jnp.concatenate(rows, 0)
     for c in range(box.shape[0]):
-        box[c, pl.ds(base, ROWS), :] = rows[:, c * 128 : (c + 1) * 128]
+        box[c, pl.ds(base, rows.shape[0]), :] = rows[:, c * 128 : (c + 1) * 128]
+
+
+def matrix_rows(e, g, g_end, k, a):
+    return [e[0:1], g[0:1], g_end[0:1], k[0, 0:1], k[-1, 7:8], a[0, 0:1], a[-1, 7:8], jnp.zeros_like(e[0:1])]
+
+
+def forcing_rows(solved, b):
+    return [s[1][0:1] for s in solved] + [s[2][0:1] for s in solved] + [b[0, 0:1], b[-1, 7:8]]
 
 
 def copies(box, me, n, axis, send, recv):
     out = []
+    rows = box.shape[1] // n
     for d in range(1, n):
-        slot = box.at[:, pl.ds(pl.multiple_of(me * ROWS, ROWS), ROWS), :]
+        slot = box.at[:, pl.ds(pl.multiple_of(me * rows, ROWS), rows), :]
         out.append(
             pltpu.make_async_remote_copy(
                 src_ref=slot,
@@ -176,59 +182,68 @@
     return out
 
 
-def interface(box, n, order, me, first_out, last_out):
-    def get_part(q, c):
+def get_row(box, n, q):
+    parts = []
+    rows = box.shape[1] // n
+    for c in range(box.shape[0]):
         if n >= 8:
-            return box[c, pl.ds(q, n, stride=ROWS), :]
+            parts.append(box[c, pl.ds(q, n, stride=rows), :])
+            continue
         sub = sublane((8, 128)) % n
         out = jnp.broadcast_to(box[c, q : q + 1, :], (8, 128))
         for i in range(1, n):
-            out = jnp.where(sub == i, box[c, i * ROWS + q : i * ROWS + q + 1, :], out)
-        return out
-
-    def get(q):
-        return wide([get_part(q, c) for c in range(box.shape[0])])
-
-    e, g = get(0), get(1)
-    f = [get(2 + i) for i in range(3)]
-    g_end = get(5)
-    f_end = [get(6 + i) for i in range(3)]
-    head = [get(9 + i) for i in range(3)]
-    tail = [get(12 + i) for i in range(3)]
-    head_next = [turn(k, -1) for k in head]
-    link = 2.0 * tail[0] * head_next[0] / (tail[0] + head_next[0])
-    gain = [link, 0.5 * head_next[1], 0.5 * head_next[2]]
-    loss = [turn(link, 1), turn(0.5 * tail[1], 1), turn(0.5 * tail[2], 1)]
-    for i, which in enumerate(order):
-        f[i] = f[i] - loss[which]
-        f_end[i] = f_end[i] + gain[which]
+            out = jnp.where(sub == i, box[c, i * rows + q : i * rows + q + 1, :], out)
+        parts.append(out)
+    return wide(parts)
+
+
+def ring_factor(box, n):
+    e, g, g_end, k_head, k_tail, a_head, a_tail = [get_row(box, n, q) for q in range(7)]
+    k_next = turn(k_head, -1)
+    link = 2.0 * k_tail * k_next / (k_tail + k_next)
+    gain = [link, 0.5 * turn(a_head, -1)]
+    loss = [turn(link, 1), turn(0.5 * a_tail, 1)]
     r = 1.0 / (e + link + g_end)
     left, right = e * r, link * r
     g = g + left * g_end + turn(right * g_end, 1)
-    f = [a + left * b + turn(right * b, 1) for a, b in zip(f, f_end)]
     e = e * right
+    levels = []
     by = 1
     while by < n:
         e_left = turn(e, by)
         s = 1.0 / (e_left + e + g)
         lo, hi = e_left * s, e * s
+        levels.append((by, lo, hi))
         g = g + turn(lo * g, -by) + turn(hi * g, by)
-        f = [a + turn(lo * a, -by) + turn(hi * a, by) for a in f]
         e = e * turn(hi, -by)
         by *= 2
-    inv = 1.0 / g
-    size = g.shape[0]
-    for i in range(3):
-        v = f[i] * inv
+    return gain, loss, r, left, right, levels, 1.0 / g
+
+
+def ring_solve(box, n, skip, ring, order, me, first_out, last_out):
+    gain, loss, r, left, right, levels, inv = ring
+    f = [get_row(box, n, skip + q) for q in range(3)]
+    f_end = [get_row(box, n, skip + q) for q in range(3, 6)]
+    b_head, b_tail = get_row(box, n, skip + 6), get_row(box, n, skip + 7)
+    gain = gain + [0.5 * turn(b_head, -1)]
+    loss = loss + [turn(0.5 * b_tail, 1)]
+    size = inv.shape[0]
+    for i, which in enumerate(order):
+        end = f_end[i] + gain[which]
+        v = f[i] - loss[which] + left * end + turn(right * end, 1)
+        for by, lo, hi in levels:
+            v = v + turn(lo * v, -by) + turn(hi * v, by)
+        v = v * inv
         first_out[i * size : (i + 1) * size, :] = v
-        last_out[i * size : (i + 1) * size, :] = r * f_end[i] + left * v + right * turn(v, -1)
+        last_out[i * size : (i + 1) * size, :] = r * end + left * v + right * turn(v, -1)
     return [
         (first_out[pl.ds(i * size + me, 1), :], last_out[pl.ds(i * size + me, 1), :]) for i in range(3)
     ]
 
 
-def kernel(nx, ny, damping, pot, lab, pri, off, out, box_x, box_y, labt, ft,
-           first_x, last_x, first_y, last_y, send_x, recv_x, send_y, recv_y):
+def kernel(nx, ny, damping, pot_hbm, lab_hbm, pri_hbm, off_hbm, out, pot, lab, pri, off, box_x, mat_y, box_y, labt, ft,
+           first_x, last_x, first_y, last_y, send_x, recv_x, send_y, recv_y,
+           send_my, recv_my, load):
     me_x, me_y = lax.axis_index("gx"), lax.axis_index("gy")
     barrier = pltpu.get_barrier_semaphore()
     for d in range(1, nx):
@@ -236,18 +251,29 @@
     for d in range(1, ny):
         pl.semaphore_signal(barrier, inc=1, device_id={"gy": lax.rem(me_y + d, ny)}, device_id_type=MESH)
 
+    loads = [
+        pltpu.make_async_copy(src, dst, load.at[i])
+        for i, (src, dst) in enumerate(((lab_hbm, lab), (pri_hbm, pri), (off_hbm, off), (pot_hbm, pot)))
+    ]
+    for copy in loads:
+        copy.start()
     def tab(row, phase):
-        return pri[row, phase] if row < 2 else off[row - 2, phase]
+        ref, row = (pri, row) if row < 2 else (off, row - 2)
+        return ref[row : row + 1, phase : phase + 1]
 
     rows, cols = lab.shape
     steps = rows // 8
+    for copy in loads[:3]:
+        copy.wait()
     labels = strided(lab, steps)
-    k, a, b = lookup(tab, 0, labels), lookup(tab, 2, labels), lookup(tab, 3, labels)
+    k, a = lookup(tab, 0, labels), lookup(tab, 2, labels)
     e = faces(k)
     levels, e_in, g, g_end = factor(e, damping)
+    b = lookup(tab, 3, labels)
     source = [e - preceding(e)[0], central(a), central(b)]
+    loads[3].wait()
     solved = [forward(levels, damping * strided(pot.at[i], steps) + source[i]) for i in range(3)]
-    put_record(box_x, me_x, e_in, g, g_end, [s[1] for s in solved], [s[2] for s in solved], [k, a, b])
+    put_record(box_x, me_x, matrix_rows(e_in, g, g_end, k, a) + forcing_rows(solved, b))
     pl.semaphore_wait(barrier, nx - 1 + ny - 1)
     sent_x = copies(box_x, me_x, nx, "gx", send_x, recv_x)
     for copy in sent_x:
@@ -268,23 +294,31 @@
     ky, ay, by = lookup(tab, 1, labels_y), lookup(tab, 2, labels_y), lookup(tab, 4, labels_y)
     ey = faces(ky)
     levels_y, ey_in, gy, gy_end = factor(ey, damping)
+    put_record(mat_y, me_y, matrix_rows(ey_in, gy, gy_end, ky, ay))
+    sent_my = copies(mat_y, me_y, ny, "gy", send_my, recv_my)
+    for copy in sent_my:
+        copy.start()
     source_y = [central(ay), ey - preceding(ey)[0], central(by)]
 
     for copy in sent_x:
         copy.wait_recv()
-    ends = interface(box_x, nx, (0, 1, 2), me_x, first_x, last_x)
+    ring_x = ring_factor(box_x, nx)
+    ends = ring_solve(box_x, nx, ROWS, ring_x, (0, 1, 2), me_x, first_x, last_x)
     solved_y = []
     for i in range(3):
         half = backward(levels, solved[i][0], *ends[i])
         put_wide(ft.at[i], across(half))
         solved_y.append(forward(levels_y, damping * strided_wide(ft.at[i], ysteps) + source_y[i]))
-    put_record(box_y, me_y, ey_in, gy, gy_end, [s[1] for s in solved_y], [s[2] for s in solved_y], [ky, ay, by])
+    put_record(box_y, me_y, forcing_rows(solved_y, by))
     sent_y = copies(box_y, me_y, ny, "gy", send_y, recv_y)
     for copy in sent_y:
         copy.start()
+    for copy in sent_my:
+        copy.wait_recv()
+    ring_y = ring_factor(mat_y, ny)
     for copy in sent_y:
         copy.wait_recv()
-    ends = interface(box_y, ny, (1, 0, 2), me_y, first_y, last_y)
+    ends = ring_solve(box_y, ny, 0, ring_y, (1, 0, 2), me_y, first_y, last_y)
     for i in range(3):
         v = backward(levels_y, solved_y[i][0], *ends[i])
         for t in range(ysteps):
@@ -293,7 +327,7 @@
         back = jnp.concatenate([ft[i, c].T for c in range(lanes // 128)], 0)[:rows].reshape(steps, 8, cols)
         for t in range(steps):
             out[i, pl.ds(t, 8, stride=steps), :] = back[t]
-    for copy in sent_x + sent_y:
+    for copy in sent_x + sent_my + sent_y:
         copy.wait_send()
 
 
@@ -303,14 +337,19 @@
     lanes = max(rows, 128)
     damping = 2.0 / (cols * cols)
     vmem = pl.BlockSpec(memory_space=pltpu.VMEM)
-    smem = pl.BlockSpec(memory_space=pltpu.SMEM)
+    hbm = pl.BlockSpec(memory_space=pltpu.HBM)
     result = pl.pallas_call(
         functools.partial(kernel, nx, ny, damping),
         out_shape=jax.ShapeDtypeStruct((loads, rows, cols), jnp.float32),
-        in_specs=[vmem, vmem, smem, smem],
+        in_specs=[hbm] * 4,
         out_specs=vmem,
         scratch_shapes=[
-            pltpu.VMEM((1, nx * ROWS, cols), jnp.float32),
+            pltpu.VMEM((loads, rows, cols), jnp.float32),
+            pltpu.VMEM((rows, cols), jnp.int32),
+            pltpu.VMEM(principal.shape, jnp.float32),
+            pltpu.VMEM(off_diagonal.shape, jnp.float32),
+            pltpu.VMEM((1, nx * 2 * ROWS, cols), jnp.float32),
+            pltpu.VMEM((lanes // 128, ny * ROWS, 128), jnp.float32),
             pltpu.VMEM((lanes // 128, ny * ROWS, 128), jnp.float32),
             pltpu.VMEM((lanes // 128, cols, 128), jnp.int32),
             pltpu.VMEM((loads, lanes // 128, cols, 128), jnp.float32),
@@ -322,6 +361,9 @@
             pltpu.SemaphoreType.DMA((nx,)),
             pltpu.SemaphoreType.DMA((ny,)),
             pltpu.SemaphoreType.DMA((ny,)),
+            pltpu.SemaphoreType.DMA((ny,)),
+            pltpu.SemaphoreType.DMA((ny,)),
+            pltpu.SemaphoreType.DMA((4,)),
         ],
         compiler_params=pltpu.CompilerParams(
             collective_id=0, has_side_effects=True, vmem_limit_bytes=32 * 1024 * 1024

time: 17.8 us -> 16.9 us (0.949)
  Pallas kernels: 14.3 us -> 13.3 us
    pallas_call x1, Pallas kernels: 14.3 us -> 13.3 us  [local(): pl.pallas_call(functools.partial(kernel, nx, ny, damping), out_shape=jax....]
where the time goes in v2:
time: 16.9 us; the launch traced here: 16.7 us
  Pallas kernels  13.3 us (79%)
  local copies, waits for them, and re-layouts  3.34 us (20%)
    pallas_call x1, Pallas kernels, local(): pl.pallas_call(functools.partial(kernel, nx, ny, damping), out_shape=jax....  13.3 us
    unnamed x9, local copies, waits for them, and re-layouts  3.34 us

profile of v2, /device:TPU:0, one launch (start us, length us, event | category | flops | bytes accessed | tf_op | source)
XLA Modules:
  0.0 16.7 jit_solution(6182928685543763620)
XLA Ops:
  0.0 0.0 copy-start.2
  0.0 0.0 copy-start.3
  0.0 0.7 %copy-done.2 = f32[3,8]{1,0:T(4,128)S(1)} copy-done((f32[3,8]{1,0:T(4,128)S(1)}, f32[3,8]{1,0:T(4,128)}, u32[]{:S(2)}) %copy-start.2) | copy-done | bytes 120
  0.7 0.0 copy-done.3
  0.7 0.0 copy-start
  0.7 1.0 %copy-done = f32[3,1,256,128]{3,2,1,0:T(8,128)S(1)} copy-done((f32[3,1,256,128]{3,2,1,0:T(8,128)S(1)}, f32[3,1,256,128]{3,2,1,0:T(8,128)}, u32[]{:S(2)}) %copy-start) | copy-done | bytes 393240
  1.7 0.0 copy-start.1
  1.7 0.9 %copy-done.1 = s32[1,256,128]{2,1,0:T(8,128)S(1)} copy-done((s32[1,256,128]{2,1,0:T(8,128)S(1)}, s32[1,256,128]{2,1,0:T(8,128)}, u32[]{:S(2)}) %copy-start.1) | copy-done | bytes 131096
  2.6 13.3 %shard_map.46 = f32[3,256,128]{2,1,0:T(8,128)S(1)} custom-call(f32[3,256,128]{2,1,0:T(8,128)S(1)} %bitcast.6, s32[256,128]{1,0:T(8,128)S(1)} %bitcast.7, f32[2,8]{1,0:T(2,128)S(1)} %copy-done.3, f32[3,8]{1,0:T(4,128)S(1)} %copy-done.2), custom_call_target="tpu_custom_call" | custom-call | tf_op jit(solution)/shard_map/pallas_call | solution.py:341
  15.9 0.7 %copy.7 = f32[3,1,256,128]{3,2,1,0:T(8,128)} copy(f32[3,1,256,128]{3,2,1,0:T(8,128)S(1)} %bitcast.5) | data formatting | bytes 786432
Async XLA Ops:
  0.0 0.7 %copy-start.2 = (f32[3,8]{1,0:T(4,128)S(1)}, f32[3,8]{1,0:T(4,128)}, u32[]{:S(2)}) copy-start(f32[3,8]{1,0:T(4,128)} %off_hbm.1) | copy-start | bytes 292
  0.0 0.7 %copy-start.3 = (f32[2,8]{1,0:T(2,128)S(1)}, f32[2,8]{1,0:T(2,128)}, u32[]{:S(2)}) copy-start(f32[2,8]{1,0:T(2,128)} %pri_hbm.1) | copy-start | bytes 196
  0.7 1.0 %copy-start = (f32[3,1,256,128]{3,2,1,0:T(8,128)S(1)}, f32[3,1,256,128]{3,2,1,0:T(8,128)}, u32[]{:S(2)}) copy-start(f32[3,1,256,128]{3,2,1,0:T(8,128)} %param.4) | copy-start | bytes 1179652
  1.7 0.9 %copy-start.1 = (s32[1,256,128]{2,1,0:T(8,128)S(1)}, s32[1,256,128]{2,1,0:T(8,128)}, u32[]{:S(2)}) copy-start(s32[1,256,128]{2,1,0:T(8,128)} %param.5) | copy-start | bytes 393220
